TPU v7x, 32 devices: a whole 2x2x4 slice. The times are simulated.
32 devices in a mesh: grp: 4 (over x, core), dev: 8 (over z, y).
Axes of the slice: x: 2, y: 2, z: 4, core: 2. Of those that a mesh axis runs over, the one named last changes fastest.
Arguments:
- traces: float32 [32, 16, 128], P(('grp', 'dev')), parts along dimension 0
- half_window: int32 [32], P(('grp', 'dev')), parts along dimension 0, may hold values from 4 to 23
- dip_slopes: int32 [9], replicated, may hold values from -4 to 4, as said below
Outputs:
- coherence: float32 [32, 16, 128], P('grp', 'dev'), parts along dimension 0
There are 4 independent parts, one for each index of `grp`. A program takes and returns all parts, laid end to end along the dimension named above; an argument that names none is the same for every part. Nothing has to cross between parts.
Inputs may be any that keep to these rules, and one draw needn't show every extreme that they name: `dip_slopes`: each trial dip is a whole number of samples per shot; both extreme dips occur.
All inputs are finite; a program needn't handle non-finite values.
Results may differ from a plain program's by a relative error of at most 0.00005.
Values sent between devices are 32-bit elements; how exact they have to be, the bound alone decides.
A program may use at most 64 MiB of HBM per device.

v0:
```python
import jax
import jax.numpy as jnp
from jax import lax
from jax.sharding import PartitionSpec as P

floor_level = 0.05


def extended_2(value, sides, width):
    for axis, dim in sides:
        size, length = (lax.axis_size(axis), value.shape[dim])
        up = [(i, (i + 1) % size) for i in range(size - 1)]
        down = [(j, i) for i, j in up]
        last = lax.slice_in_dim(value, length - width, length, axis=dim)
        initial = lax.slice_in_dim(value, 0, width, axis=dim)
        before = lax.ppermute(last, axis, up)
        after = lax.ppermute(initial, axis, down)
        value = jnp.concatenate([before, value, after], axis=dim)
    return value


def gain_control(traces, half_window):
    samples = jnp.arange(traces.shape[-1], dtype=jnp.int32)
    distance = jnp.abs(samples[:, None] - samples[None, :])
    window_mask = (distance[None, :, :] <= half_window[:, None, None]).astype(jnp.float32)
    window_count = jnp.sum(window_mask, axis=1)
    power_sum = jnp.einsum(
        "srt,stu->sru", traces * traces, window_mask, precision=lax.Precision.HIGHEST
    )
    mean_square = power_sum / window_count[:, None, :]
    return traces * lax.rsqrt(jnp.maximum(mean_square, floor_level))


def semblance_scan(widened, dip_slopes):
    shot_count = widened.shape[0]
    wide = widened.shape[1]
    length = widened.shape[2]
    inner = wide - 4
    padded = jnp.pad(widened, ((2, 2), (0, 0), (13, 13)))
    extended = length + 10
    later = jnp.arange(extended, dtype=jnp.int32)[:, None]
    earlier = jnp.arange(length, dtype=jnp.int32)[None, :]
    lag_gap = later - earlier
    time_band = ((lag_gap >= 0) & (lag_gap <= 10)).astype(jnp.float32)
    coherent = None
    for which in range(dip_slopes.shape[0]):
        slope = dip_slopes[which]
        stacked = jnp.zeros((shot_count, wide, extended), jnp.float32)
        energy_sum = jnp.zeros((shot_count, wide, extended), jnp.float32)
        for member in range(5):
            offset = member - 2
            rows = padded[member : member + shot_count, :, :]
            start = 8 + offset * slope
            shifted = lax.dynamic_slice_in_dim(rows, start, extended, 2)
            stacked = stacked + shifted
            energy_sum = energy_sum + shifted * shifted
        squared = stacked * stacked
        squared_rows = squared[:, 0:inner, :]
        energy_rows = energy_sum[:, 0:inner, :]
        for across in range(1, 5):
            squared_rows = squared_rows + squared[:, across : across + inner, :]
            energy_rows = energy_rows + energy_sum[:, across : across + inner, :]
        numerator = jnp.dot(
            squared_rows.reshape(shot_count * inner, extended),
            time_band,
            precision=lax.Precision.HIGHEST,
            preferred_element_type=jnp.float32,
        )
        denominator = jnp.dot(
            energy_rows.reshape(shot_count * inner, extended),
            time_band,
            precision=lax.Precision.HIGHEST,
            preferred_element_type=jnp.float32,
        )
        current = (numerator / (5.0 * denominator + 1.0)).reshape(shot_count, inner, length)
        coherent = current if coherent is None else jnp.maximum(coherent, current)
    return coherent


def body(traces, half_window, dip_slopes):
    balanced = gain_control(traces, half_window)
    gathered = lax.all_to_all(balanced, "dev", split_axis=1, concat_axis=0, tiled=True)
    widened = extended_2(gathered, (("dev", 1),), 2)
    return semblance_scan(widened, dip_slopes)


def solution(mesh):
    return jax.shard_map(
        body,
        mesh=mesh,
        in_specs=(P(("grp", "dev"), None, None), P(("grp", "dev")), P()),
        out_specs=P("grp", "dev", None),
        check_vma=False,
    )
```

profile of v0, /device:TPU:0, one launch (start us, length us, event | category | flops | bytes accessed | tf_op | source)
XLA Modules:
  0.0 51.2 jit_solution(14853539897846402921)
XLA Ops:
  0.7 1.5 %fusion.29 = f32[1,16,128]{2,1,0:T(8,128)} fusion(f32[1,16,128]{2,1,0:T(8,128)} %param.3, s32[]{:T(128)} %bitcast.104, f32[128]{0:T(128)S(1)} %convert_reduce_fusion), kind=kOutput, calls=%fused_computation.39 | convolution fusion | flops 3203072 | bytes 16900 | tf_op jit(solution)/shard_map/srt,stu->sru/dot_general | solution.py:27
  2.2 7.4 %all-to-all-start = ((f32[1,16,128]{2,0,1:T(1,128)}), f32[1,16,128]{2,0,1:T(1,128)S(1)}, u32[]{:S(2)}, u32[]{:S(2)}) async-start(f32[1,16,128]{2,0,1:T(1,128)} %bitcast.4), calls=%async_computation | async-start | bytes 16384 | tf_op jit(solution)/shard_map/all_to_all | solution.py:82
  9.7 0.7 %fusion.105 = (s32[1]{0:T(128)}, s32[1]{0:T(128)}, s32[1]{0:T(128)}, s32[1]{0:T(128)}, s32[1]{0:T(128)}, /*index=5*/s32[1]{0:T(128)}, s32[1]{0:T(128)}, s32[1]{0:T(128)}, s32[1]{0:T(128)}) fusion(s32[9]{0:T(128)S(1)} %copy-done), kind=kLoop, calls=%fused_computation.196 | loop fusion | bytes 72 | tf_op jit(solution)/shard_map/slice | solution.py:47
  32.6 1.3 %collective-permute-start.1 = (f32[8,2,128]{2,1,0:T(2,128)S(1)}, f32[8,2,128]{2,1,0:T(2,128)S(1)}, u32[]{:S(2)}, u32[]{:S(2)}) collective-permute-start(f32[8,2,128]{2,1,0:T(2,128)S(1)} %bitcast.106), channel_id=1, source_target_pairs={{1,0},{2,1},{3,2},{4,3},{5,4},{6,5},{7,6},{9,8},{10,9},{11,10},{12... | collective-permute-start | bytes 24584 | tf_op jit(solution)/shard_map/ppermute | solution.py:17
  33.9 4.5 %collective-permute-start = (f32[8,2,128]{2,1,0:T(2,128)S(1)}, f32[8,2,128]{2,1,0:T(2,128)S(1)}, u32[]{:S(2)}, u32[]{:S(2)}) collective-permute-start(f32[8,2,128]{2,1,0:T(2,128)S(1)} %bitcast.107), channel_id=1, source_target_pairs={{0,1},{1,2},{2,3},{3,4},{4,5},{5,6},{6,7},{8,9},{9,10},{10,11},{11... | collective-permute-start | bytes 24584 | tf_op jit(solution)/shard_map/ppermute | solution.py:16
  44.6 0.1 select_maximum_fusion
  44.7 0.3 add_multiply_fusion.6
  45.1 0.1 fusion.63
  45.2 0.3 multiply_add_fusion
  45.7 0.1 fusion.60
  45.9 0.1 slice_add_fusion
  46.0 0.1 fusion.57
  46.1 0.3 add_multiply_fusion
  46.5 0.3 add_multiply_fusion.3
  46.9 0.1 fusion.54
  47.1 0.1 slice_add_fusion.4
  47.3 0.1 fusion.51
  47.4 0.3 multiply_add_fusion.1
  47.8 0.1 fusion.48
  48.1 0.2 add_multiply_fusion.1
  48.4 0.1 fusion.45
  48.6 0.1 fusion.42
  48.8 0.1 fusion.39
  49.0 0.1 fusion.25
  49.2 0.2 fusion.23
  49.4 0.2 fusion.20
  49.5 0.2 fusion.17
  49.7 0.2 fusion.14
  49.9 0.2 fusion.11
  50.1 0.2 fusion.8
  50.2 0.2 fusion.5
  50.4 0.8 %fusion.2 = f32[16,128]{1,0:T(8,128)} fusion(f32[16,128]{1,0:T(8,128)S(1)} %fusion.5, f32[16,128]{1,0:T(8,128)S(1)} %fusion.39, f32[16,138]{1,0:T(8,128)S(1)} %reshape.379), kind=kOutput, calls=%fused_computation.3 | convolution fusion | flops 3470336 | bytes 33408 | tf_op jit(solution)/shard_map/dot_general | solution.py:69
  (35 shorter events, 0.9 us)
Async XLA Ops:
  2.2 7.4 %copy-start = (s32[9]{0:T(128)S(1)}, s32[9]{0:T(128)}, u32[]{:S(2)}) copy-start(s32[9]{0:T(128)} %param.5) | copy-start | bytes 112
  2.2 30.3 %all-to-all-start = ((f32[1,16,128]{2,0,1:T(1,128)}), f32[1,16,128]{2,0,1:T(1,128)S(1)}, u32[]{:S(2)}, u32[]{:S(2)}) async-start(f32[1,16,128]{2,0,1:T(1,128)} %bitcast.4), calls=%async_computation | async-start | bytes 16384 | tf_op jit(solution)/shard_map/all_to_all | solution.py:82
  32.6 12.0 %collective-permute-start.1 = (f32[8,2,128]{2,1,0:T(2,128)S(1)}, f32[8,2,128]{2,1,0:T(2,128)S(1)}, u32[]{:S(2)}, u32[]{:S(2)}) collective-permute-start(f32[8,2,128]{2,1,0:T(2,128)S(1)} %bitcast.106), channel_id=1, source_target_pairs={{1,0},{2,1},{3,2},{4,3},{5,4},{6,5},{7,6},{9,8},{10,9},{11,10},{12... | collective-permute-start | bytes 24584 | tf_op jit(solution)/shard_map/ppermute | solution.py:17
  33.9 10.7 %collective-permute-start = (f32[8,2,128]{2,1,0:T(2,128)S(1)}, f32[8,2,128]{2,1,0:T(2,128)S(1)}, u32[]{:S(2)}, u32[]{:S(2)}) collective-permute-start(f32[8,2,128]{2,1,0:T(2,128)S(1)} %bitcast.107), channel_id=1, source_target_pairs={{0,1},{1,2},{2,3},{3,4},{4,5},{5,6},{6,7},{8,9},{9,10},{10,11},{11... | collective-permute-start | bytes 24584 | tf_op jit(solution)/shard_map/ppermute | solution.py:16
where the time goes:
time: 51.9 us; the launch traced here: 51.2 us
  between operations  29.4 us (57%)
  starting transfers between devices  13.3 us (26%)
  matrix products  4.8 us (9%)
  other arithmetic  2.68 us (5%)
  local copies, waits for them, and re-layouts  1.05 us (2%)
    all_to_all x1, starting transfers between devices, body(): lax.all_to_all(balanced, 'dev', split_axis=1, concat_axis=0, tiled=True)  7.41 us
    ppermute x1, starting transfers between devices, extended_2(): before = lax.ppermute(last, axis, up)  4.55 us
    dot_general x9, matrix products, semblance_scan(): jnp.dot(energy_rows.reshape(shot_count * inner, extended), time_band, pre...  2.05 us
    dot_general x1, matrix products, gain_control(): jnp.einsum('srt,stu->sru', traces * traces, window_mask, precision=lax.Pr...  1.54 us
    ppermute x1, starting transfers between devices, extended_2(): after = lax.ppermute(initial, axis, down)  1.29 us
    mul x4, other arithmetic, semblance_scan(): squared = stacked * stacked  1.22 us
    dot_general x9, matrix products, semblance_scan(): jnp.dot(squared_rows.reshape(shot_count * inner, extended), time_band, pr...  1.21 us
  transfers between devices with their start and end apart: 3, of which 0 were waited for; matrix products, arithmetic and copies ran while one was open for 1% of the time, Pallas kernels for 0%

commit v1 on v0

--- a/solution.py
+++ b/solution.py
@@ -78,8 +78,20 @@
 
 
 def body(traces, half_window, dip_slopes):
+
+    def resolve_clusters(panel):
+        return jnp.concatenate(
+            jax.lax.all_to_all(
+                jnp.stack(jnp.split(panel, jax.lax.axis_size("dev"), axis=1)),
+                "dev",
+                split_axis=0,
+                concat_axis=0,
+            ),
+            axis=0,
+        )
+
     balanced = gain_control(traces, half_window)
-    gathered = lax.all_to_all(balanced, "dev", split_axis=1, concat_axis=0, tiled=True)
+    gathered = resolve_clusters(balanced)
     widened = extended_2(gathered, (("dev", 1),), 2)
     return semblance_scan(widened, dip_slopes)
 

time: 51.9 us -> 55.8 us (1.075)
  local copies, waits for them, and re-layouts: 1.05 us -> 5.57 us
  matrix products: 4.8 us -> 4.18 us
    unnamed x2 -> x9, local copies, waits for them, and re-layouts: 0.01 us -> 3.96 us
    dot_general x1, matrix products: 1.54 us -> 0.92 us  [gain_control(): jnp.einsum('srt,stu->sru', traces * traces, window_mask, precision=lax.Pr...]
    another operation x0 -> x1, local copies, waits for them, and re-layouts: none -> 0.56 us  [resolve_clusters(): jnp.stack(jnp.split(panel, jax.lax.axis_size('dev'), axis=1))]
where the time goes in v1:
time: 55.8 us; the launch traced here: 55.1 us
  between operations  29.4 us (53%)
  starting transfers between devices  13.3 us (24%)
  local copies, waits for them, and re-layouts  5.57 us (10%)
  matrix products  4.18 us (7%)
  other arithmetic  2.68 us (5%)
    all_to_all x1, starting transfers between devices, resolve_clusters(): jax.lax.all_to_all(jnp.stack(jnp.split(panel, jax.lax.axis_size('dev'), a...  7.41 us
    ppermute x1, starting transfers between devices, extended_2(): before = lax.ppermute(last, axis, up)  4.55 us
    unnamed x9, local copies, waits for them, and re-layouts  3.96 us
    dot_general x9, matrix products, semblance_scan(): jnp.dot(energy_rows.reshape(shot_count * inner, extended), time_band, pre...  2.05 us
    ppermute x1, starting transfers between devices, extended_2(): after = lax.ppermute(initial, axis, down)  1.29 us
    mul x4, other arithmetic, semblance_scan(): squared = stacked * stacked  1.22 us
    dot_general x9, matrix products, semblance_scan(): jnp.dot(squared_rows.reshape(shot_count * inner, extended), time_band, pr...  1.21 us
  transfers between devices with their start and end apart: 3, of which 0 were waited for; matrix products, arithmetic and copies ran while one was open for 1% of the time, Pallas kernels for 0%

profile of v1, /device:TPU:0, one launch (start us, length us, event | category | flops | bytes accessed | tf_op | source)
XLA Modules:
  0.0 55.1 jit_solution(9277628737639971283)
XLA Ops:
  0.7 0.9 %fusion.29 = f32[1,16,128]{2,1,0:T(8,128)S(1)} fusion(f32[1,16,128]{2,1,0:T(8,128)} %param.3, s32[]{:T(128)} %bitcast.135, f32[128]{0:T(128)S(1)} %convert_reduce_fusion), kind=kOutput, calls=%fused_computation.39 | convolution fusion | flops 3203072 | bytes 16900 | tf_op jit(solution)/shard_map/srt,stu->sru/dot_general | solution.py:27
  1.6 0.6 %constant_dynamic-update-slice_fusion.7 = f32[8,1,2,128]{3,2,1,0:T(2,128)} fusion(f32[1,16,128]{2,1,0:T(8,128)S(1)} %fusion.29), kind=kLoop, calls=%fused_computation.92 | loop fusion | bytes 2048
  2.2 0.6 %constant_dynamic-update-slice_fusion.6 = f32[8,1,2,128]{3,2,1,0:T(2,128)} fusion(f32[8,1,2,128]{3,2,1,0:T(2,128)} %constant_dynamic-update-slice_fusion.7, f32[1,16,128]{2,1,0:T(8,128)S(1)} %fusion.29), kind=kLoop, calls=%fused_computation.91 | loop fusion | bytes 2048
  2.8 0.6 %constant_dynamic-update-slice_fusion.5 = f32[8,1,2,128]{3,2,1,0:T(2,128)} fusion(f32[8,1,2,128]{3,2,1,0:T(2,128)} %constant_dynamic-update-slice_fusion.6, f32[1,16,128]{2,1,0:T(8,128)S(1)} %fusion.29), kind=kLoop, calls=%fused_computation.90 | loop fusion | bytes 2048
  3.3 0.6 %constant_dynamic-update-slice_fusion.4 = f32[8,1,2,128]{3,2,1,0:T(2,128)} fusion(f32[8,1,2,128]{3,2,1,0:T(2,128)} %constant_dynamic-update-slice_fusion.5, f32[1,16,128]{2,1,0:T(8,128)S(1)} %fusion.29), kind=kLoop, calls=%fused_computation.89 | loop fusion | bytes 2048
  3.9 0.6 %constant_dynamic-update-slice_fusion.3 = f32[8,1,2,128]{3,2,1,0:T(2,128)} fusion(f32[8,1,2,128]{3,2,1,0:T(2,128)} %constant_dynamic-update-slice_fusion.4, f32[1,16,128]{2,1,0:T(8,128)S(1)} %fusion.29), kind=kLoop, calls=%fused_computation.88 | loop fusion | bytes 2048
  4.5 0.6 %constant_dynamic-update-slice_fusion.2 = f32[8,1,2,128]{3,2,1,0:T(2,128)} fusion(f32[8,1,2,128]{3,2,1,0:T(2,128)} %constant_dynamic-update-slice_fusion.3, f32[1,16,128]{2,1,0:T(8,128)S(1)} %fusion.29), kind=kLoop, calls=%fused_computation.87 | loop fusion | bytes 2048
  5.0 0.6 %constant_dynamic-update-slice_fusion.1 = f32[8,1,2,128]{3,2,1,0:T(2,128)} fusion(f32[8,1,2,128]{3,2,1,0:T(2,128)} %constant_dynamic-update-slice_fusion.2, f32[1,16,128]{2,1,0:T(8,128)S(1)} %fusion.29), kind=kLoop, calls=%fused_computation.86 | loop fusion | bytes 2048
  5.6 0.6 %constant_dynamic-update-slice_fusion = f32[8,1,2,128]{3,2,1,0:T(2,128)} fusion(f32[8,1,2,128]{3,2,1,0:T(2,128)} %constant_dynamic-update-slice_fusion.1, f32[1,16,128]{2,1,0:T(8,128)S(1)} %fusion.29), kind=kLoop, calls=%fused_computation.85 | loop fusion | bytes 2048 | tf_op jit(solution)/shard_map/stack | solution.py:85
  6.2 7.4 %all-to-all-start = ((f32[8,1,2,128]{3,2,1,0:T(2,128)}), f32[8,1,2,128]{3,2,1,0:T(2,128)S(1)}, u32[]{:S(2)}, u32[]{:S(2)}) async-start(f32[8,1,2,128]{3,2,1,0:T(2,128)} %constant_dynamic-update-slice_fusion), calls=%async_computation | async-start | bytes 16384 | tf_op jit(solution)/shard_map/all_to_all | solution.py:84
  13.6 0.7 %fusion.105 = (s32[1]{0:T(128)}, s32[1]{0:T(128)}, s32[1]{0:T(128)}, s32[1]{0:T(128)}, s32[1]{0:T(128)}, /*index=5*/s32[1]{0:T(128)}, s32[1]{0:T(128)}, s32[1]{0:T(128)}, s32[1]{0:T(128)}) fusion(s32[9]{0:T(128)S(1)} %copy-done), kind=kLoop, calls=%fused_computation.212 | loop fusion | bytes 72 | tf_op jit(solution)/shard_map/slice | solution.py:47
  36.5 1.3 %collective-permute-start.1 = (f32[8,2,128]{2,1,0:T(2,128)S(1)}, f32[8,2,128]{2,1,0:T(2,128)S(1)}, u32[]{:S(2)}, u32[]{:S(2)}) collective-permute-start(f32[8,2,128]{2,1,0:T(2,128)S(1)} %bitcast.137), channel_id=1, source_target_pairs={{1,0},{2,1},{3,2},{4,3},{5,4},{6,5},{7,6},{9,8},{10,9},{11,10},{12... | collective-permute-start | bytes 24584 | tf_op jit(solution)/shard_map/ppermute | solution.py:17
  37.8 4.5 %collective-permute-start = (f32[8,2,128]{2,1,0:T(2,128)S(1)}, f32[8,2,128]{2,1,0:T(2,128)S(1)}, u32[]{:S(2)}, u32[]{:S(2)}) collective-permute-start(f32[8,2,128]{2,1,0:T(2,128)S(1)} %bitcast.138), channel_id=1, source_target_pairs={{0,1},{1,2},{2,3},{3,4},{4,5},{5,6},{6,7},{8,9},{9,10},{10,11},{11... | collective-permute-start | bytes 24584 | tf_op jit(solution)/shard_map/ppermute | solution.py:16
  48.7 0.3 add_multiply_fusion.6
  49.2 0.3 multiply_add_fusion
  49.9 0.1 fusion.57
  50.1 0.3 add_multiply_fusion
  50.5 0.3 add_multiply_fusion.3
  50.8 0.1 fusion.54
  51.2 0.1 fusion.51
  51.3 0.3 multiply_add_fusion.1
  52.0 0.2 add_multiply_fusion.1
  52.6 0.1 fusion.42
  52.9 0.1 fusion.25
  53.1 0.2 fusion.23
  53.3 0.2 fusion.20
  53.5 0.2 fusion.17
  53.6 0.2 fusion.14
  53.8 0.2 fusion.11
  54.0 0.2 fusion.8
  54.2 0.2 fusion.5
  54.3 0.8 %fusion.2 = f32[16,128]{1,0:T(8,128)} fusion(f32[16,128]{1,0:T(8,128)S(1)} %fusion.5, f32[16,128]{1,0:T(8,128)S(1)} %fusion.39, f32[16,138]{1,0:T(8,128)S(1)} %reshape.380), kind=kOutput, calls=%fused_computation.3 | convolution fusion | flops 3470336 | bytes 33408 | tf_op jit(solution)/shard_map/dot_general | solution.py:69
  (43 shorter events, 1.8 us)
Async XLA Ops:
  6.1 7.4 %copy-start = (s32[9]{0:T(128)S(1)}, s32[9]{0:T(128)}, u32[]{:S(2)}) copy-start(s32[9]{0:T(128)} %param.5) | copy-start | bytes 112
  6.2 30.3 %all-to-all-start = ((f32[8,1,2,128]{3,2,1,0:T(2,128)}), f32[8,1,2,128]{3,2,1,0:T(2,128)S(1)}, u32[]{:S(2)}, u32[]{:S(2)}) async-start(f32[8,1,2,128]{3,2,1,0:T(2,128)} %constant_dynamic-update-slice_fusion), calls=%async_computation | async-start | bytes 16384 | tf_op jit(solution)/shard_map/all_to_all | solution.py:84
  36.5 12.0 %collective-permute-start.1 = (f32[8,2,128]{2,1,0:T(2,128)S(1)}, f32[8,2,128]{2,1,0:T(2,128)S(1)}, u32[]{:S(2)}, u32[]{:S(2)}) collective-permute-start(f32[8,2,128]{2,1,0:T(2,128)S(1)} %bitcast.137), channel_id=1, source_target_pairs={{1,0},{2,1},{3,2},{4,3},{5,4},{6,5},{7,6},{9,8},{10,9},{11,10},{12... | collective-permute-start | bytes 24584 | tf_op jit(solution)/shard_map/ppermute | solution.py:17
  37.8 10.7 %collective-permute-start = (f32[8,2,128]{2,1,0:T(2,128)S(1)}, f32[8,2,128]{2,1,0:T(2,128)S(1)}, u32[]{:S(2)}, u32[]{:S(2)}) collective-permute-start(f32[8,2,128]{2,1,0:T(2,128)S(1)} %bitcast.138), channel_id=1, source_target_pairs={{0,1},{1,2},{2,3},{3,4},{4,5},{5,6},{6,7},{8,9},{9,10},{10,11},{11... | collective-permute-start | bytes 24584 | tf_op jit(solution)/shard_map/ppermute | solution.py:16
